TPU v7x, 32 devices: a whole 2x2x4 slice. The times are simulated.
32 devices in a mesh: page: 2 (over y), blk: 8 (over z, x), head: 2 (over core).
Axes of the slice: x: 2, y: 2, z: 4, core: 2. Of those that a mesh axis runs over, the one named last changes fastest.
Arguments:
- vis_tokens: bfloat16 [2, 1152, 768], P('page', 'blk'), may hold values from -6 to 6
- query_tokens: bfloat16 [2, 256, 768], P('page'), may hold values from -6 to 6
- answer_lengths: int32 [2], P('page'), may hold values from 5 to 256, as said below
- norm_gains: float32 [6, 768], replicated, may hold values from 0.1 to 1.9
- bias_table: float32 [12, 23, 23], P('head'), may hold values from -4 to 4
- window_qkv: bfloat16 [3, 768, 768], P(None, None, 'head'), may hold values from -0.3125 to 0.3125
- window_out: bfloat16 [768, 768], P('head'), may hold values from -0.21875 to 0.21875
- causal_qkv: bfloat16 [3, 768, 768], P(None, None, 'head'), may hold values from -0.3125 to 0.3125
- causal_out: bfloat16 [768, 768], P('head'), may hold values from -0.3125 to 0.3125
- read_qkv: bfloat16 [3, 768, 768], P(None, None, 'head'), may hold values from -0.3125 to 0.3125
- read_out: bfloat16 [768, 768], P('head'), may hold values from -0.875 to 0.875
- write_qkv: bfloat16 [3, 768, 768], P(None, None, 'head'), may hold values from -0.3125 to 0.3125
- write_out: bfloat16 [768, 768], P('head'), may hold values from -0.4375 to 0.4375
- vis_up: bfloat16 [768, 3072], P(None, 'head'), may hold values from -0.21875 to 0.21875
- vis_down: bfloat16 [3072, 768], P('head'), may hold values from -0.109375 to 0.109375
- query_up: bfloat16 [768, 3072], P(None, 'head'), may hold values from -0.21875 to 0.21875
- query_down: bfloat16 [3072, 768], P('head'), may hold values from -0.109375 to 0.109375
- cot_vis: bfloat16 [2, 1152, 768], P('page', 'blk'), may hold values from -6 to 6
- cot_query: bfloat16 [2, 256, 768], P('page'), may hold values from -6 to 6
Outputs:
- vis_out: bfloat16 [2, 1152, 768], P('page', 'blk')
- query_out: bfloat16 [2, 256, 768], P('page')
- grad_visual: float32 [2, 1152, 768], P('page', 'blk')
- grad_query: float32 [2, 256, 768], P('page')
- grad_gains: float32 [6, 768], P(None, ('page', 'blk'))
- grad_table: float32 [12, 23, 23], P('head')
- grad_window_qkv: float32 [3, 768, 768], P(None, ('page', 'blk'), 'head')
- grad_window_out: float32 [768, 768], P('head', ('page', 'blk'))
- grad_causal_qkv: float32 [3, 768, 768], P(None, ('page', 'blk'), 'head')
- grad_causal_out: float32 [768, 768], P('head', ('page', 'blk'))
- grad_read_qkv: float32 [3, 768, 768], P(None, ('page', 'blk'), 'head')
- grad_read_out: float32 [768, 768], P('head', ('page', 'blk'))
- grad_write_qkv: float32 [3, 768, 768], P(None, ('page', 'blk'), 'head')
- grad_write_out: float32 [768, 768], P('head', ('page', 'blk'))
- grad_vis_up: float32 [768, 3072], P(('page', 'blk'), 'head')
- grad_vis_down: float32 [3072, 768], P('head', ('page', 'blk'))
- grad_query_up: float32 [768, 3072], P(('page', 'blk'), 'head')
- grad_query_down: float32 [3072, 768], P('head', ('page', 'blk'))
Inputs may be any that keep to these rules, and one draw needn't show every extreme that they name: `answer_lengths`: answer length of each page; some page has all 256 query tokens live.
All inputs are finite; a program needn't handle non-finite values.
Results may differ from a plain program's by a relative error of at most 0.035.
The roundings to bfloat16 on the way count: a program that leaves them out, or rounds other values in their place, can miss the bound.
Values may be sent and summed in bfloat16 or wider, within the bound.
A program may use at most 256 MiB of HBM per device.

v0:
```python
from functools import partial

import jax
import jax.numpy as jnp
from jax import lax
from jax.sharding import PartitionSpec as P

HEAD_DIM = 64
WIN = 12


EPS = 1e-05
HIGH = lax.Precision.HIGHEST
exact_gelu = partial(jax.nn.gelu, approximate=False)


def combined_all(value, axis, join):
    pieces = jax.tree.map(lambda part: lax.all_gather(part, axis), value)
    head = jax.tree.map(lambda part: part[0], pieces)
    tail = jax.tree.map(lambda part: part[1:], pieces)
    subtotal, _ = lax.scan(lambda subtotal, section: (join(subtotal, section), None), head, tail)
    return subtotal


def matmul(matrix, other):
    return jnp.dot(matrix, other, preferred_element_type=jnp.float32)


def times_back(matrix, other):
    return lax.dot_general(
        matrix, other, (((1,), (1,)), ((), ())), preferred_element_type=jnp.float32
    )


def inner_rows(matrix, other):
    return lax.dot_general(
        matrix, other, (((0,), (0,)), ((), ())), preferred_element_type=jnp.float32
    )


def layer_norm(stream, gain):
    centred = stream - jnp.mean(stream, axis=-1, keepdims=True)
    inverse = lax.rsqrt(jnp.mean(centred * centred, axis=-1, keepdims=True) + EPS)
    normal = centred * inverse
    return (normal * gain, normal, inverse)


def norm_back(grad_out, normal, inverse, gain):
    scaled = grad_out * gain
    return inverse * (
        scaled
        - jnp.mean(scaled, axis=-1, keepdims=True)
        - normal * jnp.mean(scaled * normal, axis=-1, keepdims=True)
    )


def scores_of(queries, keyset, factor):
    return (
        jnp.einsum("bqhe,bkhe->bhqk", queries, keyset, preferred_element_type=jnp.float32) * factor
    )


def attend(queries, keyset, values, additive, factor):
    scores = scores_of(queries, keyset, factor) + additive
    peak_val = jnp.max(scores, axis=-1, keepdims=True)
    log_total = peak_val + jnp.log(jnp.sum(jnp.exp(scores - peak_val), axis=-1, keepdims=True))
    soft_probs = jnp.exp(scores - log_total).astype(jnp.bfloat16)
    mix_out = jnp.einsum("bhqk,bkhe->bqhe", soft_probs, values, preferred_element_type=jnp.float32)
    return (mix_out, log_total)


def attend_back(grad_low, queries, keyset, values, additive, log_total, factor, reduce_rows):
    scores = scores_of(queries, keyset, factor) + additive
    soft_probs = jnp.exp(scores - log_total)
    grad_probs = jnp.einsum("bqhe,bkhe->bhqk", grad_low, values, preferred_element_type=jnp.float32)
    grad_values = jnp.einsum(
        "bhqk,bqhe->bkhe",
        soft_probs.astype(jnp.bfloat16),
        grad_low,
        preferred_element_type=jnp.float32,
    )
    rowdot = reduce_rows(jnp.sum(soft_probs * grad_probs, axis=-1, keepdims=True))
    grad_scores = soft_probs * (grad_probs - rowdot)
    rounded = grad_scores.astype(jnp.bfloat16)
    grad_queries = (
        jnp.einsum("bhqk,bkhe->bqhe", rounded, keyset, preferred_element_type=jnp.float32) * factor
    )
    grad_keys = (
        jnp.einsum("bhqk,bqhe->bkhe", rounded, queries, preferred_element_type=jnp.float32) * factor
    )
    return (grad_queries, grad_keys, grad_values, grad_scores)


def join_softmax(earlier, later):
    peak_val = jnp.maximum(earlier[0], later[0])
    return (
        peak_val,
        earlier[1] * jnp.exp(earlier[0] - peak_val) + later[1] * jnp.exp(later[0] - peak_val),
    )


def feed_back(grad_out, normed_low, hidden, act_low, up_weight, down_weight, select):
    grad_low = grad_out.astype(jnp.bfloat16)
    grad_act = times_back(grad_low, down_weight)
    grad_down = inner_rows(select(act_low), select(grad_low))
    (grad_hidden,) = jax.vjp(exact_gelu, hidden)[1](grad_act)
    hidden_low = grad_hidden.astype(jnp.bfloat16)
    grad_up = inner_rows(select(normed_low), select(hidden_low))
    return (times_back(hidden_low, up_weight), grad_up, grad_down)


def shards(
    vis_tokens,
    query_tokens,
    answer_lengths,
    norm_gains,
    bias_table,
    window_qkv,
    window_out,
    causal_qkv,
    causal_out,
    read_qkv,
    read_out,
    write_qkv,
    write_out,
    vis_up,
    vis_down,
    query_up,
    query_down,
    cot_vis,
    cot_query,
):
    factor = HEAD_DIM ** (-0.5)
    vis_in = vis_tokens[0].astype(jnp.float32)
    query_in = query_tokens[0].astype(jnp.float32)
    length = answer_lengths[0]
    vis_rows = vis_in.shape[0]
    query_rows = query_in.shape[0]
    local_heads = window_out.shape[0] // HEAD_DIM
    win_area = WIN * WIN
    windows = vis_rows // win_area
    own_rows = query_rows // lax.axis_size("blk")
    first_row = lax.axis_index("blk") * own_rows

    def split(tensor, count):
        return tensor.reshape(count, -1, local_heads, HEAD_DIM)

    def project(normed_low, weight, count):
        return split(matmul(normed_low, weight).astype(jnp.bfloat16), count)

    def flat_low(tensor, count_rows):
        return tensor.reshape(count_rows, -1).astype(jnp.bfloat16)

    def own(tensor):
        return lax.dynamic_slice_in_dim(tensor, first_row, own_rows, 0)

    def same(tensor):
        return tensor

    def head_total(first_part, second_part):
        return lax.psum((first_part, second_part), "head")

    offsets = jnp.arange(WIN)
    one_hot = (
        (offsets[:, None] - offsets[None, :] + WIN - 1)[:, :, None]
        == jnp.arange(2 * WIN - 1)[None, None, :]
    ).astype(jnp.float32)
    rel_bias = jnp.einsum(
        "pqa,rsb,hab->hprqs", one_hot, one_hot, bias_table, precision=HIGH
    ).reshape(local_heads, win_area, win_area)
    window_extra = rel_bias[None]
    positions = jnp.arange(query_rows)
    causal_extra = jnp.where(
        (positions[None, :] <= positions[:, None]) & (positions[None, :] < length), 0.0, -jnp.inf
    )[None, None]
    write_extra = jnp.where(positions < length, 0.0, -jnp.inf)[None, None, None, :]
    window_norm, window_hat, window_inv = layer_norm(vis_in, norm_gains[0])
    window_low = window_norm.astype(jnp.bfloat16)
    window_query = project(window_low, window_qkv[0], windows)
    window_keys = project(window_low, window_qkv[1], windows)
    window_values = project(window_low, window_qkv[2], windows)
    window_mix, window_lse = attend(window_query, window_keys, window_values, window_extra, factor)
    window_att = flat_low(window_mix, vis_rows)
    causal_norm, causal_hat, causal_inv = layer_norm(query_in, norm_gains[1])
    causal_low = causal_norm.astype(jnp.bfloat16)
    causal_query = project(causal_low, causal_qkv[0], 1)
    causal_keys = project(causal_low, causal_qkv[1], 1)
    causal_values = project(causal_low, causal_qkv[2], 1)
    causal_mix, causal_lse = attend(causal_query, causal_keys, causal_values, causal_extra, factor)
    causal_att = flat_low(causal_mix, query_rows)
    window_sum, causal_sum = head_total(
        matmul(window_att, window_out), matmul(causal_att, causal_out)
    )
    vis_one = vis_in + window_sum
    query_one = query_in + causal_sum
    cross_query_norm, cross_query_hat, cross_query_inv = layer_norm(query_one, norm_gains[2])
    cross_query_low = cross_query_norm.astype(jnp.bfloat16)
    cross_vis_norm, cross_vis_hat, cross_vis_inv = layer_norm(vis_one, norm_gains[3])
    cross_vis_low = cross_vis_norm.astype(jnp.bfloat16)
    read_query = project(cross_query_low, read_qkv[0], 1)
    read_keys = project(cross_vis_low, read_qkv[1], 1)
    read_values = project(cross_vis_low, read_qkv[2], 1)
    write_query = project(cross_vis_low, write_qkv[0], 1)
    write_keys = project(cross_query_low, write_qkv[1], 1)
    write_values = project(cross_query_low, write_qkv[2], 1)
    read_scores = scores_of(read_query, read_keys, factor)
    peak_val = jnp.max(read_scores, axis=-1, keepdims=True)
    mass = jnp.sum(jnp.exp(read_scores - peak_val), axis=-1, keepdims=True)
    peak_val, mass = combined_all((peak_val, mass), "blk", join_softmax)
    read_lse = peak_val + jnp.log(mass)
    read_probs = jnp.exp(read_scores - read_lse).astype(jnp.bfloat16)
    read_part = jnp.einsum(
        "bhqk,bkhe->bqhe", read_probs, read_values, preferred_element_type=jnp.float32
    )
    read_att = flat_low(lax.psum(read_part, "blk"), query_rows)
    write_mix, write_lse = attend(write_query, write_keys, write_values, write_extra, factor)
    write_att = flat_low(write_mix, vis_rows)
    read_sum, write_sum = head_total(matmul(read_att, read_out), matmul(write_att, write_out))
    query_two = query_one + read_sum
    vis_two = vis_one + write_sum
    feed_vis_norm, feed_vis_hat, feed_vis_inv = layer_norm(vis_two, norm_gains[4])
    feed_vis_low = feed_vis_norm.astype(jnp.bfloat16)
    vis_hidden = matmul(feed_vis_low, vis_up)
    vis_act = exact_gelu(vis_hidden).astype(jnp.bfloat16)
    feed_query_norm, feed_query_hat, feed_query_inv = layer_norm(query_two, norm_gains[5])
    feed_query_low = feed_query_norm.astype(jnp.bfloat16)
    query_hidden = matmul(feed_query_low, query_up)
    query_act = exact_gelu(query_hidden).astype(jnp.bfloat16)
    vis_feed, query_feed = head_total(matmul(vis_act, vis_down), matmul(query_act, query_down))
    vis_three = vis_two + vis_feed
    query_three = query_two + query_feed
    grad_vis3 = cot_vis[0].astype(jnp.float32)
    grad_query3 = cot_query[0].astype(jnp.float32)
    vis_back, vis_up_grad, vis_down_grad = feed_back(
        grad_vis3, feed_vis_low, vis_hidden, vis_act, vis_up, vis_down, same
    )
    query_back, query_up_grad, query_down_grad = feed_back(
        grad_query3, feed_query_low, query_hidden, query_act, query_up, query_down, own
    )
    vis_back, query_back = head_total(vis_back, query_back)
    grad_vis2 = grad_vis3 + norm_back(vis_back, feed_vis_hat, feed_vis_inv, norm_gains[4])
    grad_query2 = grad_query3 + norm_back(query_back, feed_query_hat, feed_query_inv, norm_gains[5])
    gain_feed_vis = jnp.sum(vis_back * feed_vis_hat, axis=0)
    gain_feed_query = jnp.sum(own(query_back) * own(feed_query_hat), axis=0)
    vis2_low = grad_vis2.astype(jnp.bfloat16)
    query2_low = grad_query2.astype(jnp.bfloat16)
    read_out_grad = inner_rows(own(read_att), own(query2_low))
    write_out_grad = inner_rows(write_att, vis2_low)
    read_grad_att = split(times_back(query2_low, read_out).astype(jnp.bfloat16), 1)
    write_grad_att = split(times_back(vis2_low, write_out).astype(jnp.bfloat16), 1)
    write_dq, write_dk, write_dv, write_ds = attend_back(
        write_grad_att, write_query, write_keys, write_values, write_extra, write_lse, factor, same
    )

    def partial_rows(rowdot):
        return lax.psum(rowdot, "blk")

    read_dq, read_dk, read_dv, read_ds = attend_back(
        read_grad_att, read_query, read_keys, read_values, 0.0, read_lse, factor, partial_rows
    )
    read_dq, write_dk, write_dv = lax.psum((read_dq, write_dk, write_dv), "blk")
    read_dq_low = flat_low(read_dq, query_rows)
    read_dk_low = flat_low(read_dk, vis_rows)
    read_dv_low = flat_low(read_dv, vis_rows)
    write_dq_low = flat_low(write_dq, vis_rows)
    write_dk_low = flat_low(write_dk, query_rows)
    write_dv_low = flat_low(write_dv, query_rows)
    cross_query_back = (
        times_back(read_dq_low, read_qkv[0])
        + times_back(write_dk_low, write_qkv[1])
        + times_back(write_dv_low, write_qkv[2])
    )
    cross_vis_back = (
        times_back(read_dk_low, read_qkv[1])
        + times_back(read_dv_low, read_qkv[2])
        + times_back(write_dq_low, write_qkv[0])
    )
    read_qkv_grad = jnp.stack(
        [
            inner_rows(own(cross_query_low), own(read_dq_low)),
            inner_rows(cross_vis_low, read_dk_low),
            inner_rows(cross_vis_low, read_dv_low),
        ]
    )
    write_qkv_grad = jnp.stack(
        [
            inner_rows(cross_vis_low, write_dq_low),
            inner_rows(own(cross_query_low), own(write_dk_low)),
            inner_rows(own(cross_query_low), own(write_dv_low)),
        ]
    )
    cross_query_back, cross_vis_back = head_total(cross_query_back, cross_vis_back)
    grad_query1 = grad_query2 + norm_back(
        cross_query_back, cross_query_hat, cross_query_inv, norm_gains[2]
    )
    grad_vis1 = grad_vis2 + norm_back(cross_vis_back, cross_vis_hat, cross_vis_inv, norm_gains[3])
    gain_cross_query = jnp.sum(own(cross_query_back) * own(cross_query_hat), axis=0)
    gain_cross_vis = jnp.sum(cross_vis_back * cross_vis_hat, axis=0)
    vis1_low = grad_vis1.astype(jnp.bfloat16)
    query1_low = grad_query1.astype(jnp.bfloat16)
    window_out_grad = inner_rows(window_att, vis1_low)
    causal_out_grad = inner_rows(own(causal_att), own(query1_low))
    window_dq, window_dk, window_dv, window_ds = attend_back(
        split(times_back(vis1_low, window_out).astype(jnp.bfloat16), windows),
        window_query,
        window_keys,
        window_values,
        window_extra,
        window_lse,
        factor,
        same,
    )
    window_lows = [flat_low(tensor, vis_rows) for tensor in (window_dq, window_dk, window_dv)]
    window_qkv_grad = jnp.stack([inner_rows(window_low, member) for member in window_lows])
    window_back = (
        times_back(window_lows[0], window_qkv[0])
        + times_back(window_lows[1], window_qkv[1])
        + times_back(window_lows[2], window_qkv[2])
    )
    summed = jnp.sum(window_ds, axis=0).reshape(local_heads, WIN, WIN, WIN, WIN)
    table_grad = jnp.einsum("pqa,rsb,hprqs->hab", one_hot, one_hot, summed, precision=HIGH)
    causal_dq, causal_dk, causal_dv, causal_ds = attend_back(
        split(times_back(query1_low, causal_out).astype(jnp.bfloat16), 1),
        causal_query,
        causal_keys,
        causal_values,
        causal_extra,
        causal_lse,
        factor,
        same,
    )
    causal_lows = [flat_low(tensor, query_rows) for tensor in (causal_dq, causal_dk, causal_dv)]
    causal_qkv_grad = jnp.stack(
        [inner_rows(own(causal_low), own(member)) for member in causal_lows]
    )
    causal_back = (
        times_back(causal_lows[0], causal_qkv[0])
        + times_back(causal_lows[1], causal_qkv[1])
        + times_back(causal_lows[2], causal_qkv[2])
    )
    window_back, causal_back = head_total(window_back, causal_back)
    grad_vis0 = grad_vis1 + norm_back(window_back, window_hat, window_inv, norm_gains[0])
    grad_query0 = grad_query1 + norm_back(causal_back, causal_hat, causal_inv, norm_gains[1])
    gain_window = jnp.sum(window_back * window_hat, axis=0)
    gain_causal = jnp.sum(own(causal_back) * own(causal_hat), axis=0)
    gain_grad = jnp.stack(
        [gain_window, gain_causal, gain_cross_query, gain_cross_vis, gain_feed_vis, gain_feed_query]
    )
    (
        gains_part,
        window_qkv_part,
        window_out_part,
        causal_qkv_part,
        causal_out_part,
        read_qkv_part,
        read_out_part,
        write_qkv_part,
        write_out_part,
        vis_up_part,
        vis_down_part,
        query_up_part,
        query_down_part,
    ) = (
        lax.psum_scatter(gain_grad, ("page", "blk"), scatter_dimension=1, tiled=True),
        lax.psum_scatter(window_qkv_grad, ("page", "blk"), scatter_dimension=1, tiled=True),
        lax.psum_scatter(window_out_grad, ("page", "blk"), scatter_dimension=1, tiled=True),
        lax.psum_scatter(causal_qkv_grad, ("page", "blk"), scatter_dimension=1, tiled=True),
        lax.psum_scatter(causal_out_grad, ("page", "blk"), scatter_dimension=1, tiled=True),
        lax.psum_scatter(read_qkv_grad, ("page", "blk"), scatter_dimension=1, tiled=True),
        lax.psum_scatter(read_out_grad, ("page", "blk"), scatter_dimension=1, tiled=True),
        lax.psum_scatter(write_qkv_grad, ("page", "blk"), scatter_dimension=1, tiled=True),
        lax.psum_scatter(write_out_grad, ("page", "blk"), scatter_dimension=1, tiled=True),
        lax.psum_scatter(vis_up_grad, ("page", "blk"), scatter_dimension=0, tiled=True),
        lax.psum_scatter(vis_down_grad, ("page", "blk"), scatter_dimension=1, tiled=True),
        lax.psum_scatter(query_up_grad, ("page", "blk"), scatter_dimension=0, tiled=True),
        lax.psum_scatter(query_down_grad, ("page", "blk"), scatter_dimension=1, tiled=True),
    )
    table_part = lax.psum(table_grad, ("page", "blk"))
    return (
        vis_three.astype(jnp.bfloat16)[None],
        query_three.astype(jnp.bfloat16)[None],
        grad_vis0[None],
        grad_query0[None],
        gains_part,
        table_part,
        window_qkv_part,
        window_out_part,
        causal_qkv_part,
        causal_out_part,
        read_qkv_part,
        read_out_part,
        write_qkv_part,
        write_out_part,
        vis_up_part,
        vis_down_part,
        query_up_part,
        query_down_part,
    )


def solution(mesh):
    in_specs = (
        P("page", "blk", None),
        P("page", None, None),
        P("page"),
        P(),
        P("head", None, None),
        P(None, None, "head"),
        P("head", None),
        P(None, None, "head"),
        P("head", None),
        P(None, None, "head"),
        P("head", None),
        P(None, None, "head"),
        P("head", None),
        P(None, "head"),
        P("head", None),
        P(None, "head"),
        P("head", None),
        P("page", "blk", None),
        P("page", None, None),
    )
    out_specs = (
        P("page", "blk", None),
        P("page", None, None),
        P("page", "blk", None),
        P("page", None, None),
        P(None, ("page", "blk")),
        P("head", None, None),
        P(None, ("page", "blk"), "head"),
        P("head", ("page", "blk")),
        P(None, ("page", "blk"), "head"),
        P("head", ("page", "blk")),
        P(None, ("page", "blk"), "head"),
        P("head", ("page", "blk")),
        P(None, ("page", "blk"), "head"),
        P("head", ("page", "blk")),
        P(("page", "blk"), "head"),
        P("head", ("page", "blk")),
        P(("page", "blk"), "head"),
        P("head", ("page", "blk")),
    )
    return jax.shard_map(shards, mesh=mesh, in_specs=in_specs, out_specs=out_specs, check_vma=False)
```

profile of v0, /device:TPU:0, one launch (start us, length us, event | category | flops | bytes accessed | tf_op | source)
XLA Modules:
  0.0 2228.7 jit_solution(2092561471129013898)
XLA Ops:
  30.8 5.1 convolution_bitcast_fusion
  35.9 5.7 reshape.833
  50.5 22.2 all-reduce.22.cloned.1.call-done
  85.0 31.2 %all-gather.3 = f32[8,6,256]{2,1,0:T(8,128)S(1)} all-gather(f32[1,6,256]{2,1,0:T(8,128)S(1)} %bitcast.523), channel_id=3, replica_groups=mesh['page'=2,'blk'=8,'head'=2] {'blk'}, dimensions={0}, use_global_device_ids=true | all-gather | bytes 55296 | tf_op jit(solution)/shard_map/all_gather | solution.py:18
  116.8 30.5 %all-gather.2 = f32[8,6,256]{2,1,0:T(8,128)S(1)} all-gather(f32[1,6,256]{2,1,0:T(8,128)S(1)} %bitcast.522), channel_id=2, replica_groups=mesh['page'=2,'blk'=8,'head'=2] {'blk'}, dimensions={0}, use_global_device_ids=true | all-gather | bytes 55296 | tf_op jit(solution)/shard_map/all_gather | solution.py:18
  161.1 6.2 while.12
  169.3 43.2 %all-reduce.23 = bf16[1,256,6,64]{1,3,2,0:T(8,128)(2,1)} all-reduce(f32[1,256,6,64]{1,3,2,0:T(8,128)} %convolution_bitcast_fusion.16), channel_id=1, replica_groups=mesh['page'=2,'blk'=8,'head'=2] {'blk'}, use_global_device_ids=true, to_apply=%region_24.25 | all-reduce | flops 98304 | bytes 589824 | tf_op jit(solution)/shard_map/psum | solution.py:215
  216.6 17.3 all-reduce.20.cloned.1.call-done
  244.3 4.8 multiply_convert_fusion.1
  252.8 21.2 all-reduce.18.cloned.1.call-done
  287.0 22.0 psum.135
  312.9 71.6 %all-reduce.24 = (bf16[1,256,6,64]{1,3,2,0:T(8,128)(2,1)}, bf16[1,256,6,64]{1,3,2,0:T(8,128)(2,1)}, bf16[1,256,6,64]{1,3,2,0:T(8,128)(2,1)}) all-reduce(f32[1,256,6,64]{1,3,2,0:T(8,128)} %fusion.11, f32[1,256,6,64]{1,3,2,0:T(8,128)S(1)} %copy-done.90, ...), channel_id=1, replica_groups=mesh['page'=2,'blk'=8,'head'=2] {'blk'}, use_global_device_ids=true, to_apply=%region_45.46 | all-reduce | flops 294912 | bytes 1769472 | tf_op jit(solution)/shard_map/psum | solution.py:261
  391.4 3.1 fusion.206
  396.2 15.1 all-reduce.16.cloned.1.call-done
  433.7 21.3 all-reduce.14.cloned.1.call-done
  477.8 3.9 fusion.139
  485.8 3.9 fusion.137
  503.8 5.0 reshape.804
  508.8 8.7 convolution_bitcast_fusion.14
  518.2 78.6 %psum.143 = f32[6,23,23]{2,1,0:T(8,128)} all-reduce(f32[6,23,23]{2,1,0:T(8,128)S(1)} %convolution_bitcast_fusion.17), channel_id=1, replica_groups=mesh['page'=2,'blk'=8,'head'=2] {'page','blk'}, use_global_device_ids=true, to_apply=%region_62.63 | all-reduce | flops 3174 | bytes 25392 | tf_op jit(solution)/shard_map/psum | solution.py:378
  602.0 109.7 %reduce-scatter.26.cloned.1.call-done = f32[384,48]{0,1:T(8,128)} async-done(((f32[384,768]{0,1:T(8,128)}), f32[384,48]{0,1:T(8,128)}) %reduce-scatter.26.cloned.1.call-update) | async-done | bytes 73744 | tf_op jit(solution)/shard_map/reduce_scatter | solution.py:370
  711.7 128.5 %reduce-scatter.30.cloned.1.call-done = f32[384,48]{0,1:T(8,128)} async-done(((f32[384,768]{0,1:T(8,128)}), f32[384,48]{0,1:T(8,128)}) %reduce-scatter.30.cloned.1.call-update) | async-done | bytes 73744 | tf_op jit(solution)/shard_map/reduce_scatter | solution.py:372
  840.2 128.7 %reduce-scatter.22.cloned.1.call-done = f32[384,48]{0,1:T(8,128)} async-done(((f32[384,768]{0,1:T(8,128)}), f32[384,48]{0,1:T(8,128)}) %reduce-scatter.22.cloned.1.call-update) | async-done | bytes 73744 | tf_op jit(solution)/shard_map/reduce_scatter | solution.py:368
  968.9 128.6 %reduce-scatter.18.cloned.1.call-done = f32[384,48]{0,1:T(8,128)} async-done(((f32[384,768]{0,1:T(8,128)}), f32[384,48]{0,1:T(8,128)}) %reduce-scatter.18.cloned.1.call-update) | async-done | bytes 73744 | tf_op jit(solution)/shard_map/reduce_scatter | solution.py:366
  1097.5 138.8 %reduce-scatter.28.cloned.1.call-done = f32[3,48,384]{2,1,0:T(8,128)} async-done(((f32[3,768,384]{2,1,0:T(8,128)}), f32[3,48,384]{2,1,0:T(8,128)}) %reduce-scatter.28.cloned.1.call-update) | async-done | bytes 221200 | tf_op jit(solution)/shard_map/reduce_scatter | solution.py:371
  1236.3 138.9 %reduce-scatter.24.cloned.1.call-done = f32[3,48,384]{2,1,0:T(8,128)} async-done(((f32[3,768,384]{2,1,0:T(8,128)}), f32[3,48,384]{2,1,0:T(8,128)}) %reduce-scatter.24.cloned.1.call-update) | async-done | bytes 221200 | tf_op jit(solution)/shard_map/reduce_scatter | solution.py:369
  1375.2 142.6 %reduce-scatter.36.cloned.1.call-done = f32[48,1536]{1,0:T(8,128)} async-done(((f32[768,1536]{1,0:T(8,128)}), f32[48,1536]{1,0:T(8,128)}) %reduce-scatter.36.cloned.1.call-update) | async-done | bytes 294928 | tf_op jit(solution)/shard_map/reduce_scatter | solution.py:375
  1517.8 141.8 %reduce-scatter.32.cloned.1.call-done = f32[48,1536]{1,0:T(8,128)} async-done(((f32[768,1536]{1,0:T(8,128)}), f32[48,1536]{1,0:T(8,128)}) %reduce-scatter.32.cloned.1.call-update) | async-done | bytes 294928 | tf_op jit(solution)/shard_map/reduce_scatter | solution.py:373
  1659.6 142.9 %reduce-scatter.38.cloned.1.call-done = f32[1536,48]{0,1:T(8,128)} async-done(((f32[1536,768]{0,1:T(8,128)}), f32[1536,48]{0,1:T(8,128)}) %reduce-scatter.38.cloned.1.call-update) | async-done | bytes 294928 | tf_op jit(solution)/shard_map/reduce_scatter | solution.py:376
  1802.4 141.6 %reduce-scatter.34.cloned.1.call-done = f32[1536,48]{0,1:T(8,128)} async-done(((f32[1536,768]{0,1:T(8,128)}), f32[1536,48]{0,1:T(8,128)}) %reduce-scatter.34.cloned.1.call-update) | async-done | bytes 294928 | tf_op jit(solution)/shard_map/reduce_scatter | solution.py:374
  1944.0 138.6 %reduce-scatter.16.cloned.1.call-done = f32[3,48,384]{2,1,0:T(8,128)} async-done(((f32[3,768,384]{2,1,0:T(8,128)}), f32[3,48,384]{2,1,0:T(8,128)}) %reduce-scatter.16.cloned.1.call-update) | async-done | bytes 221200 | tf_op jit(solution)/shard_map/reduce_scatter | solution.py:365
  2082.6 138.8 %reduce-scatter.20.cloned.1.call-done = f32[3,48,384]{2,1,0:T(8,128)} async-done(((f32[3,768,384]{2,1,0:T(8,128)}), f32[3,48,384]{2,1,0:T(8,128)}) %reduce-scatter.20.cloned.1.call-update) | async-done | bytes 221200 | tf_op jit(solution)/shard_map/reduce_scatter | solution.py:367
  (521 shorter events, 177.6 us)
Async XLA Ops:
  7.2 237.1 %copy-start = (bf16[768,1536]{1,0:T(8,128)(2,1)S(1)}, bf16[768,1536]{1,0:T(8,128)(2,1)}, u32[]{:S(2)}) copy-start(bf16[768,1536]{1,0:T(8,128)(2,1)} %param.36) | copy-start | bytes 7077892
  7.2 65.5 %all-reduce.22.cloned.1.call-start = ((), (), s32[]{:S(2)}) async-start(), calls=%async_computation.30 | async-start | bytes 2457600 | tf_op jit(solution)/shard_map/psum | solution.py:161
  7.3 23.5 %copy-start.114 = (s32[12,12]{1,0:T(8,128)}, s32[12,12]{1,0:T(8,128)S(1)}, u32[]{:S(2)}) copy-start(s32[12,12]{1,0:T(8,128)S(1)} %subtract_add_fusion) | copy-start | bytes 1732
  11.3 63.0 %copy-start.118 = (f32[768]{0:T(1024)}, f32[768]{0:T(1024)S(1)}, u32[]{:S(2)}) copy-start(f32[768]{0:T(1024)S(1)} %get-tuple-element.74) | copy-start | bytes 9220
  11.3 67.0 %copy-start.122 = (f32[768]{0:T(1024)}, f32[768]{0:T(1024)S(1)}, u32[]{:S(2)}) copy-start(f32[768]{0:T(1024)S(1)} %get-tuple-element.75) | copy-start | bytes 9220
  48.8 25.2 %copy-start.51 = (bf16[6,64,144]{2,1,0:T(8,128)(2,1)}, bf16[6,64,144]{2,1,0:T(8,128)(2,1)S(1)}, u32[]{:S(2)}) copy-start(bf16[6,64,144]{2,1,0:T(8,128)(2,1)S(1)} %convolution_convert_fusion.3) | copy-start | bytes 331780
  49.9 184.0 %all-reduce.20.cloned.1.call-start = ((), (), s32[]{:S(2)}) async-start(), calls=%async_computation.29 | async-start | bytes 2457600 | tf_op jit(solution)/shard_map/psum | solution.py:161
  216.6 57.5 %all-reduce.18.cloned.1.call-start = ((), (), s32[]{:S(2)}) async-start(), calls=%async_computation.28 | async-start | bytes 2457600 | tf_op jit(solution)/shard_map/psum | solution.py:161
  252.8 158.5 %all-reduce.16.cloned.1.call-start = ((), (), s32[]{:S(2)}) async-start(), calls=%async_computation.27 | async-start | bytes 2457600 | tf_op jit(solution)/shard_map/psum | solution.py:161
  285.7 100.6 %copy-start.65 = (bf16[6,64,144]{2,1,0:T(8,128)(2,1)}, bf16[6,64,144]{2,1,0:T(8,128)(2,1)S(1)}, u32[]{:S(2)}) copy-start(bf16[6,64,144]{2,1,0:T(8,128)(2,1)S(1)} %convolution_convert_fusion.1) | copy-start | bytes 331780
  309.6 75.0 %copy-start.76 = (bf16[6,64,144]{2,1,0:T(8,128)(2,1)}, bf16[6,64,144]{2,1,0:T(8,128)(2,1)S(1)}, u32[]{:S(2)}) copy-start(bf16[6,64,144]{2,1,0:T(8,128)(2,1)S(1)} %fusion.15) | copy-start | bytes 331780
  391.1 63.8 %all-reduce.14.cloned.1.call-start = ((), (), s32[]{:S(2)}) async-start(), calls=%async_computation.26 | async-start | bytes 4915200 | tf_op jit(solution)/shard_map/psum | solution.py:161
  431.5 23.4 %copy-start.127 = (f32[144]{0:T(256)S(1)}, f32[144]{0:T(256)}, u32[]{:S(2)}) copy-start(f32[144]{0:T(256)} %copy-done.126) | copy-start | bytes 1732
  431.5 24.8 %copy-start.11 = (bf16[1,256,768]{2,1,0:T(8,128)(2,1)S(1)}, bf16[1,256,768]{2,1,0:T(8,128)(2,1)}, u32[]{:S(2)}) copy-start(bf16[1,256,768]{2,1,0:T(8,128)(2,1)} %param.22) | copy-start | bytes 1179652
  431.6 24.8 %copy-start.133 = (f32[256]{0:T(256)S(1)}, f32[256]{0:T(256)}, u32[]{:S(2)}) copy-start(f32[256]{0:T(256)} %copy-done.132) | copy-start | bytes 3076
  431.6 24.8 %copy-start.137 = (f32[256]{0:T(256)S(1)}, f32[256]{0:T(256)}, u32[]{:S(2)}) copy-start(f32[256]{0:T(256)} %copy-done.136) | copy-start | bytes 3076
  431.6 169.0 %reduce-scatter.40.cloned.1.call-start = ((), (), s32[]{:S(2)}) async-start(), calls=%async_computation.25 | async-start | bytes 417792
  459.9 251.8 %reduce-scatter.26.cloned.1.call-start = ((), (), s32[]{:S(2)}) async-start(), calls=%async_computation.18 | async-start | bytes 1253376 | tf_op jit(solution)/shard_map/reduce_scatter | solution.py:370
  462.2 378.0 %reduce-scatter.30.cloned.1.call-start = ((), (), s32[]{:S(2)}) async-start(), calls=%async_computation.20 | async-start | bytes 1253376 | tf_op jit(solution)/shard_map/reduce_scatter | solution.py:372
  463.8 505.1 %reduce-scatter.22.cloned.1.call-start = ((), (), s32[]{:S(2)}) async-start(), calls=%async_computation.16 | async-start | bytes 1253376 | tf_op jit(solution)/shard_map/reduce_scatter | solution.py:368
  466.2 631.4 %reduce-scatter.18.cloned.1.call-start = ((), (), s32[]{:S(2)}) async-start(), calls=%async_computation.14 | async-start | bytes 1253376 | tf_op jit(solution)/shard_map/reduce_scatter | solution.py:366
  467.8 768.5 %reduce-scatter.28.cloned.1.call-start = ((), (), s32[]{:S(2)}) async-start(), calls=%async_computation.19 | async-start | bytes 3760128 | tf_op jit(solution)/shard_map/reduce_scatter | solution.py:371
  473.2 902.0 %reduce-scatter.24.cloned.1.call-start = ((), (), s32[]{:S(2)}) async-start(), calls=%async_computation.17 | async-start | bytes 3760128 | tf_op jit(solution)/shard_map/reduce_scatter | solution.py:369
  477.7 1040.1 %reduce-scatter.36.cloned.1.call-start = ((), (), s32[]{:S(2)}) async-start(), calls=%async_computation.23 | async-start | bytes 5013504 | tf_op jit(solution)/shard_map/reduce_scatter | solution.py:375
  481.7 1177.9 %reduce-scatter.32.cloned.1.call-start = ((), (), s32[]{:S(2)}) async-start(), calls=%async_computation.21 | async-start | bytes 5013504 | tf_op jit(solution)/shard_map/reduce_scatter | solution.py:373
  485.7 1316.7 %reduce-scatter.38.cloned.1.call-start = ((), (), s32[]{:S(2)}) async-start(), calls=%async_computation.24 | async-start | bytes 5013504 | tf_op jit(solution)/shard_map/reduce_scatter | solution.py:376
  489.6 1454.4 %reduce-scatter.34.cloned.1.call-start = ((), (), s32[]{:S(2)}) async-start(), calls=%async_computation.22 | async-start | bytes 5013504 | tf_op jit(solution)/shard_map/reduce_scatter | solution.py:374
  493.8 1588.8 %reduce-scatter.16.cloned.1.call-start = ((), (), s32[]{:S(2)}) async-start(), calls=%async_computation.13 | async-start | bytes 3760128 | tf_op jit(solution)/shard_map/reduce_scatter | solution.py:365
  498.4 1723.0 %reduce-scatter.20.cloned.1.call-start = ((), (), s32[]{:S(2)}) async-start(), calls=%async_computation.15 | async-start | bytes 3760128 | tf_op jit(solution)/shard_map/reduce_scatter | solution.py:367
  508.8 88.1 %copy-start.112 = (f32[144,768]{1,0:T(8,128)S(1)}, f32[144,768]{1,0:T(8,128)}, u32[]{:S(2)}) copy-start(f32[144,768]{1,0:T(8,128)} %get-tuple-element.92) | copy-start | bytes 1327108
  517.5 80.0 %copy-start.79 = (f32[144,768]{1,0:T(8,128)S(1)}, f32[144,768]{1,0:T(8,128)}, u32[]{:S(2)}) copy-start(f32[144,768]{1,0:T(8,128)} %get-tuple-element.94) | copy-start | bytes 1327108
  598.6 1622.9 %copy-start.1 = (bf16[768,1536]{1,0:T(8,128)(2,1)S(1)}, bf16[768,1536]{1,0:T(8,128)(2,1)}, u32[]{:S(2)}) copy-start(bf16[768,1536]{1,0:T(8,128)(2,1)} %param.36) | copy-start | bytes 7077892
  (128 other events, 465.5 us)
Sparse Core Ops, SparseCore 0:
  50.0 22.6 all-reduce.21
  216.7 17.1 all-reduce.19
  252.9 21.1 all-reduce.17
  391.3 20.0 all-reduce.15
  431.7 23.2 all-reduce.13
  460.0 122.8 reduce-scatter.39
  588.9 122.7 reduce-scatter.25
  717.7 122.4 reduce-scatter.29
  846.3 122.5 reduce-scatter.21
  974.8 122.6 reduce-scatter.17
  1104.0 132.2 reduce-scatter.27
  1242.7 132.4 reduce-scatter.23
  1381.7 136.0 reduce-scatter.35
  1523.4 136.1 reduce-scatter.31
  1666.0 136.4 reduce-scatter.37
  1808.0 135.9 reduce-scatter.33
  1950.4 132.2 reduce-scatter.15
  2088.9 132.4 reduce-scatter.19
where the time goes:
time: 2240 us; the launch traced here: 2230 us
  waiting for transfers between devices  1720 us (77%)
  blocking collectives  277 us (12%)
  matrix products  116 us (5%)
  local copies, waits for them, and re-layouts  54.5 us (2%)
  other arithmetic  45.2 us (2%)
    reduce_scatter x1, waiting for transfers between devices, shards(): lax.psum_scatter(query_down_grad, ('page', 'blk'), scatter_dimension=1, t...  143 us
    reduce_scatter x1, waiting for transfers between devices, shards(): lax.psum_scatter(query_up_grad, ('page', 'blk'), scatter_dimension=0, til...  143 us
    reduce_scatter x1, waiting for transfers between devices, shards(): lax.psum_scatter(vis_up_grad, ('page', 'blk'), scatter_dimension=0, tiled...  142 us
    reduce_scatter x1, waiting for transfers between devices, shards(): lax.psum_scatter(vis_down_grad, ('page', 'blk'), scatter_dimension=1, til...  142 us
    reduce_scatter x1, waiting for transfers between devices, shards(): lax.psum_scatter(read_qkv_grad, ('page', 'blk'), scatter_dimension=1, til...  139 us
    reduce_scatter x1, waiting for transfers between devices, shards(): lax.psum_scatter(causal_qkv_grad, ('page', 'blk'), scatter_dimension=1, t...  139 us
    reduce_scatter x1, waiting for transfers between devices, shards(): lax.psum_scatter(write_qkv_grad, ('page', 'blk'), scatter_dimension=1, ti...  139 us
    reduce_scatter x1, waiting for transfers between devices, shards(): lax.psum_scatter(window_qkv_grad, ('page', 'blk'), scatter_dimension=1, t...  139 us
  transfers between devices with their start and end apart: 18, of which 17 were waited for; matrix products, arithmetic and copies ran while one was open for 3% of the time, Pallas kernels for 0%

commit v1 on v0

--- a/solution.py
+++ b/solution.py
@@ -3,6 +3,8 @@
 import jax
 import jax.numpy as jnp
 from jax import lax
+from jax.experimental import pallas as pl
+from jax.experimental.pallas import tpu as pltpu
 from jax.sharding import PartitionSpec as P
 
 HEAD_DIM = 64
@@ -12,6 +14,835 @@
 EPS = 1e-05
 HIGH = lax.Precision.HIGHEST
 exact_gelu = partial(jax.nn.gelu, approximate=False)
+
+MESH = pl.DeviceIdType.MESH
+BF = jnp.bfloat16
+F32 = jnp.float32
+DIFFS = 2 * WIN - 1
+AREA = WIN * WIN
+TABLE_LANES = 640
+STRIP_LANES = 384
+
+
+def mm(a, b):
+    return jnp.dot(a, b, preferred_element_type=F32)
+
+
+def mm_nt(a, b, precision=None):
+    return lax.dot_general(a, b, (((1,), (1,)), ((), ())), precision=precision, preferred_element_type=F32)
+
+
+def mm_tn(a, b):
+    return lax.dot_general(a, b, (((0,), (0,)), ((), ())), preferred_element_type=F32)
+
+
+def iota(shape, axis):
+    return lax.broadcasted_iota(jnp.int32, shape, axis)
+
+
+def loop(count, body, unroll=1):
+    def step(i, carry):
+        body(i)
+        return carry
+
+    lax.fori_loop(0, count, step, 0, unroll=unroll)
+
+
+def row_loop(count, step, body):
+    loop(count // step, lambda i: body(pl.ds(pl.multiple_of(i * step, step), step)))
+
+
+def row_sum(count, step, width, body):
+    def add(i, total):
+        value = body(pl.ds(pl.multiple_of(i * step, step), step))
+        return total + value.reshape(step // 8, 8, width).sum(0)
+
+    total = lax.fori_loop(0, count // step, add, jnp.zeros((8, width), F32))
+    return jnp.sum(total, axis=0, keepdims=True)
+
+
+class Names:
+    def __init__(self, **entries):
+        self.__dict__.update(entries)
+
+
+def scratch_shapes(R, Q, D, H, F, nb, own, cut):
+    heads = H // HEAD_DIM
+    nz = nb // 2
+    half = D // 2
+    B, S = BF, F32
+    return dict(
+        w_win=((3, D, H), B), w_win_out=((H, D), B), w_cau=((3, D, H), B), w_cau_out=((H, D), B),
+        w_read=((3, D, H), B), w_read_out=((H, D), B), w_write=((3, D, H), B), w_write_out=((H, D), B),
+        w_up=((D, F), B), w_down=((F, D), B),
+        win_low=((R, D), B), win_inv=((R, 128), S), cau_low=((Q, D), B), cau_inv=((Q, 128), S),
+        cq_low=((Q, D), B), cq_hat=((Q, D), S), cq_inv=((Q, 128), S),
+        cv_low=((R, D), B), cv_hat=((R, D), S), cv_inv=((R, 128), S),
+        fv_low=((R, D), B), fv_hat=((R, D), S), fv_inv=((R, 128), S),
+        fq_low=((Q, D), B), fq_hat=((Q, D), S), fq_inv=((Q, 128), S),
+        vis1=((R, D), S), vis2=((R, D), S), que1=((Q, D), S), que2=((Q, D), S),
+        gvis2_low=((R, D), B), gvis1_low=((R, D), B), gque2_low=((Q, D), B), gque1_low=((Q, D), B),
+        win_qkv=((3, R, H), B), cau_qkv=((3, Q, H), B),
+        read_q=((Q, H), B), read_kv=((2, R, H), B), write_q=((R, H), B), write_kv=((2, Q, H), B),
+        win_p=((heads, R, R), S), cau_p=((heads, Q, Q), S), read_p=((heads, Q, R), S), write_p=((heads, R, Q), S),
+        da_v=((R, H), B), da_q=((Q, H), B),
+        bias=((heads, R, R), S), strip=((heads, 16, STRIP_LANES), S), rolled=((heads, 16, TABLE_LANES), S),
+        hot=((STRIP_LANES, TABLE_LANES), B),
+        a_q=((Q, D), S), a_q_in=((Q, D), S), a_v=((R, D), S), a_v_in=((R, D), S),
+        b_q=((Q, D), S), b_q_in=((Q, D), S), b_v=((R, D), S), b_v_in=((R, D), S),
+        part=((Q, H + 128), S), part_in=((nb - 1, own, H + 128), S), mix=((Q, H + 128), S),
+        read_att=((Q, H), B), cau_att=((Q, H), B),
+        qg=((Q, 3 * H), S), qg_in=((nb - 1, own, 3 * H), S), qg_low=((Q, 3 * H), B),
+        cau_g=((Q, 3 * H), B),
+        dyq=((Q, 2 * F), B),
+        dyf=((R, 2 * F), B), dyf_in=((R, 2 * F), B), dyc=((R, 4 * H), B), dyc_in=((R, 4 * H), B),
+        dyw=((R, 4 * H), B), dyw_in=((R, 4 * H), B),
+        sel=((2, half, D), B), sel_q=((2 * cut, D), B),
+        xf=((2, half, R), B), xf_in=((2, half, R), B), xc=((2, half, R), B), xc_in=((2, half, R), B),
+        xw=((2, half, R), B), xw_in=((2, half, R), B), x_out=((2, half, R), B),
+        gf_in=((2 * F // D, half // 2, D), B), zf_in=((nz - 1, cut, 2 * F), B),
+        gc_in=((4 * H // D, half // 2, D), B), zc_in=((nz - 1, cut, 4 * H), B),
+        gw_in=((4 * H // D, half // 2, D), B), zw_in=((nz - 1, cut, 4 * H), B),
+        tf=((cut, 2 * F), B), tf_in=((cut, 2 * F), B), tc=((cut, 4 * H), B), tc_in=((cut, 4 * H), B),
+        tw=((cut, 4 * H), B), tw_in=((cut, 4 * H), B),
+        gain=((8, D), S), gain_in=((8, D), S), gain_page=((8, D), S), gain_blk=((nb - 1, 8, D), S),
+        tab=((8, TABLE_LANES), S), tab_in=((8, TABLE_LANES), S), tab_page=((8, TABLE_LANES), S),
+        tab_blk=((nb - 1, 8, TABLE_LANES), S),
+        slab_v=((cut, 2 * F + 8 * H), S), slab_q=((cut, 2 * F + 8 * H), S),
+    )
+
+
+WEIGHTS = ("w_win", "w_win_out", "w_cau", "w_cau_out", "w_read", "w_read_out", "w_write", "w_write_out", "w_vup", "w_vdown", "w_qup", "w_qdown")
+LOAD_ORDER = ("w_cau", "w_cau_out", "w_win", "w_win_out", "w_read", "w_write", "w_write_out", "w_read_out", "w_vdown", "w_vup")
+FEED_REFS = dict(w_vup="w_up", w_qup="w_up", w_vdown="w_down", w_qdown="w_down")
+
+
+def block_kernel(
+    names, nb, vis_ref, query_ref, length_ref, gains_ref, table_ref, cotv_ref, cotq_ref, *rest
+):
+    hbm = dict(zip(WEIGHTS, rest[:12]))
+    vis_out, query_out, grad_vis, grad_query, gain_out, table_out, out_v, out_q = rest[12:20]
+    s = Names(**dict(zip(names, rest[20 : 20 + len(names)])))
+    send_sem, recv_sem, load_sem, out_sem = rest[20 + len(names) :]
+
+    R, D = vis_ref.shape
+    Q = query_ref.shape[0]
+    H = s.w_win_out.shape[0]
+    F = s.w_up.shape[1]
+    heads = H // HEAD_DIM
+    pairs = heads // 2
+    nz = nb // 2
+    own = Q // nb
+    cut = D // (2 * nb)
+    half = D // 2
+
+    p, b, h = lax.axis_index("page"), lax.axis_index("blk"), lax.axis_index("head")
+    z, x = b // 2, b % 2
+    core = (p, b, 1 - h)
+    page = (1 - p, b, h)
+    side = (p, z * 2 + (1 - x), h)
+    peers = [(p, lax.rem(b + step, nb), h) for step in range(1, nb)]
+    line = [(p, lax.rem(z + step, nz) * 2 + x, h) for step in range(1, nz)]
+
+    loads = {}
+
+    def load(name):
+        target = getattr(s, FEED_REFS.get(name, name))
+        loads[name] = pltpu.make_async_copy(hbm[name], target, load_sem.at[len(loads)])
+        loads[name].start()
+
+    for name in LOAD_ORDER:
+        load(name)
+    barrier = pltpu.get_barrier_semaphore()
+    for device in [core, page] + peers:
+        pl.semaphore_signal(barrier, inc=1, device_id=device, device_id_type=MESH)
+
+    count = [0]
+
+    def push(src, dst, device):
+        at = count[0]
+        count[0] += 1
+        copy = pltpu.make_async_remote_copy(
+            src_ref=src, dst_ref=dst, send_sem=send_sem.at[at], recv_sem=recv_sem.at[at], device_id=device, device_id_type=MESH
+        )
+        copy.start()
+        return copy
+
+    started = []
+
+    def send(src, dst, device):
+        copy = push(src, dst, device)
+        started.append(copy)
+        return copy
+
+    def sent(copy):
+        started[:] = [other for other in started if other is not copy]
+        copy.wait_send()
+
+    written = []
+
+    def write(src, dst):
+        copy = pltpu.make_async_copy(src, dst, out_sem.at[len(written)])
+        copy.start()
+        written.append(copy)
+
+    lane = iota((1, 128), 1)
+    first = lane < HEAD_DIM
+    keep = [jnp.where(first, 1.0, 0.0).astype(BF), jnp.where(first, 0.0, 1.0).astype(BF)]
+    factor = HEAD_DIM ** (-0.5)
+    scaled = [jnp.where(first, factor, 0.0).astype(BF), jnp.where(first, 0.0, factor).astype(BF)]
+
+    def columns(j, width=128):
+        if isinstance(j, int):
+            return pl.ds(j * width, width)
+        return pl.ds(pl.multiple_of(j * width, width), width)
+
+    def pair_loop(body):
+        for j in range(pairs):
+            body(j)
+
+
+    def norm(count, step, stream, gain_row, low, hat, inv, keep_ref=None):
+        gain = gains_ref[gain_row : gain_row + 1, :]
+
+        def body(ds):
+            rows = stream(ds)
+            if keep_ref is not None:
+                keep_ref[ds, :] = rows
+            middle = jnp.mean(rows, axis=-1, keepdims=True)
+            centred = rows - middle
+            inverse = lax.rsqrt(jnp.mean(centred * centred, axis=-1, keepdims=True) + EPS)
+            normal = centred * inverse
+            if hat is not None:
+                hat[ds, :] = normal
+            inv[ds, :] = jnp.where(first, inverse, middle)
+            low[ds, :] = (normal * gain).astype(BF)
+
+        row_loop(count, step, body)
+
+    def norm_grad(count, step, before, parts, gain_row, hat, inv, out, low=None):
+        gain = gains_ref[gain_row : gain_row + 1, :]
+
+        def body(ds):
+            back = parts[0][ds, :] + parts[1][ds, :]
+            normal = hat(ds) if callable(hat) else hat[ds, :]
+            grown = back * gain
+            even = jnp.mean(grown, axis=-1, keepdims=True)
+            along = jnp.mean(grown * normal, axis=-1, keepdims=True)
+            total = before(ds) + inv[ds, 0:1] * (grown - even - normal * along)
+            out[ds, :] = total
+            if low is not None:
+                low[ds, :] = total.astype(BF)
+            return back * normal
+
+        s.gain[gain_row : gain_row + 1, :] = row_sum(count, step, D, body)
+
+    def attend(q, k, v, extra, probs, out):
+        def pair(j):
+            at = columns(j)
+            qp, kp, vp = q[:, at], k[:, at], v[:, at]
+            halves = []
+            for t in range(2):
+                scores = extra(mm_nt(qp * scaled[t], kp), 2 * j + t)
+                raised = jnp.exp(scores - jnp.max(scores, axis=-1, keepdims=True))
+                prob = raised * (1.0 / jnp.sum(raised, axis=-1, keepdims=True))
+                probs[2 * j + t] = prob
+                halves.append(mm(prob.astype(BF), vp))
+            out[:, at] = jnp.where(first, halves[0], halves[1]).astype(BF)
+
+        pair_loop(pair)
+
+    def attend_back(q, k, v, da, prob_of, put, rowdot=None, hook=None):
+        def pair(j):
+            at = columns(j)
+            qp, kp, vp, dap = q[:, at], k[:, at], v[:, at], da[:, at]
+            dq = dk = dv = None
+            for t in range(2):
+                prob = prob_of(2 * j + t)
+                own_da = dap * keep[t]
+                dprob = mm_nt(own_da, vp)
+                if rowdot is None:
+                    delta = jnp.sum(prob * dprob, axis=-1, keepdims=True)
+                else:
+                    delta = rowdot(dap, j, t)
+                ds = prob * (dprob - delta)
+                if hook is not None:
+                    hook(2 * j + t, ds)
+                low = ds.astype(BF)
+                parts = (mm(low, kp * scaled[t]), mm_tn(low, qp * scaled[t]), mm_tn(prob.astype(BF), own_da))
+                dq, dk, dv = parts if dq is None else (dq + parts[0], dk + parts[1], dv + parts[2])
+            put(at, dq, dk, dv)
+
+        pair_loop(pair)
+
+    def feed(low, cot, up, down, dy):
+        width = 256
+
+        def body(c):
+            at = columns(c, width)
+            hidden = mm(low[...], up[:, at])
+            grad_act = mm_nt(cot[...], down[at, :])
+            spread = 0.5 + 0.5 * lax.erf(hidden * (0.5**0.5))
+            bell = jnp.exp(-0.5 * hidden * hidden) * 0.3989422804014327
+            dy[:, columns(c + F // width, width)] = (hidden * spread).astype(BF)
+            dy[:, at] = (grad_act * (spread + hidden * bell)).astype(BF)
+
+        loop(F // width, body)
+
+    def left(pieces, mine):
+        for at, piece in enumerate(pieces):
+            s.x_out[at] = mm_nt(s.sel[1], piece[...]).astype(BF)
+            mine[at] = mm_nt(s.sel[0], piece[...]).astype(BF)
+
+    def weight_grads(mine, other, dy, dy_in, split, panels):
+        for n, panel in enumerate(panels):
+            width = 384
+            for c in range(D // width):
+                low = n * D + c * width
+                at = 0 if low < split else 1
+                cols = pl.ds(low, width)
+                value = mm(mine[at], dy[:, cols]) + mm(other[at], dy_in[:, cols])
+                panel[:, pl.ds(c * width, width)] = value.astype(BF)
+
+    def side_push(panels, incoming):
+        theirs = pl.ds(pl.multiple_of((1 - x) * (half // 2), half // 2), half // 2)
+        return [send(panel.at[theirs], incoming.at[n], side) for n, panel in enumerate(panels)]
+
+    def block_rows(at):
+        return pl.ds(pl.multiple_of(at * cut, cut), cut)
+
+    def line_push(panels, incoming, out, arrive):
+        copies = []
+        for step in range(1, nz):
+            to = lax.rem(z + step, nz)
+            rows = pl.ds((step - 1) * cut, cut)
+            for n, panel in enumerate(panels):
+                total = panel[block_rows(x * nz + to), :].astype(F32) + incoming[n, block_rows(to), :].astype(F32)
+                out[rows, pl.ds(n * D, D)] = total.astype(BF)
+            copies.append(send(out.at[rows], arrive.at[step - 1], line[step - 1]))
+        return copies
+
+    def line_sum(panels, incoming, arrive, offset):
+        for n, panel in enumerate(panels):
+            total = panel[block_rows(x * nz + z), :].astype(F32) + incoming[n, block_rows(z), :].astype(F32)
+            for step in range(1, nz):
+                total = total + arrive[step - 1, :, pl.ds(n * D, D)].astype(F32)
+            s.slab_v[:, pl.ds(offset + n * D, D)] = total
+        section = pl.ds(offset, D * len(panels))
+        write(s.slab_v.at[:, section], out_v.at[:, section])
+
+    def query_grads(piece, dy, dy_at, size, offset, out, out_at):
+        turned = mm_nt(s.sel_q[...], piece[...]).astype(BF)
+        width = 384
+        for c in range(size // width):
+            value = mm(turned, dy[:, pl.ds(dy_at + c * width, width)])
+            s.slab_q[:, pl.ds(offset + c * width, width)] = value[:cut]
+            out[:, pl.ds(out_at + c * width, width)] = value[cut:].astype(BF)
+
+    def add_query(arrive, offset):
+        width = 768
+        size = arrive.shape[1]
+        for c in range(size // width):
+            s.slab_q[:, pl.ds(offset + c * width, width)] += arrive[:, pl.ds(c * width, width)].astype(F32)
+        section = pl.ds(offset, size)
+        write(s.slab_q.at[:, section], out_q.at[:, section])
+
+    def split_dot(product, values, ones):
+        total = None
+        for _ in range(3):
+            part = values.astype(BF)
+            values = values - part.astype(F32)
+            share = product(part, ones)
+            total = share if total is None else total + share
+        return total
+
+    def store(ref, ds, value):
+        ref[ds, :] = value.astype(ref.dtype)
+
+    RV, RQ = 48, 32
+
+    for at, start in enumerate((p * half, (1 - p) * half)):
+        for place in range(nb):
+            block = (place % nz) * 2 + place // nz
+            rows = pl.ds(place * cut, cut)
+            s.sel[at, rows, :] = (iota((cut, D), 1) == iota((cut, D), 0) + (start + block * cut)).astype(BF)
+    rows = iota((2 * cut, D), 0)
+    start = jnp.where(rows < cut, (p * nb + b) * cut, ((1 - p) * nb + b) * cut - cut)
+    s.sel_q[...] = (iota((2 * cut, D), 1) == rows + start).astype(BF)
+
+    index = iota((STRIP_LANES, 1), 0)
+    outer = ((index.astype(F32) + 0.5) * (1.0 / WIN)).astype(jnp.int32)
+    target = (2 * WIN - 2 - outer) * DIFFS + (WIN - 1) - (index - outer * WIN)
+    target = jnp.where(index < DIFFS * WIN, target, -1)
+    s.hot[...] = (iota((STRIP_LANES, TABLE_LANES), 1) == target).astype(BF)
+    s.rolled[...] = jnp.zeros(s.rolled.shape, F32)
+    for px in range(WIN):
+        turned = table_ref[...] if px == 0 else pltpu.roll(table_ref[...], TABLE_LANES - px, 1)
+        for head in range(heads):
+            s.rolled[head, px : px + 1, :] = turned[head : head + 1, :]
+    for head in range(heads):
+        s.strip[head] = split_dot(mm_nt, s.rolled[head], s.hot[...])
+    for py in range(WIN):
+        at = (WIN - 1 - py) * WIN
+        s.bias[:, py * WIN : (py + 1) * WIN, :] = s.strip[:, 0:WIN, at : at + AREA]
+
+    position = iota((1, Q), 1)
+    alive = position < length_ref[0]
+    norm(Q, RQ, lambda ds: query_ref[ds, :].astype(F32), 1, s.cau_low, None, s.cau_inv)
+    loads["w_cau"].wait()
+    for i in range(3):
+        s.cau_qkv[i] = mm(s.cau_low[...], s.w_cau[i]).astype(BF)
+    causal_live = (iota((Q, Q), 1) <= iota((Q, Q), 0)) & alive
+    attend(
+        s.cau_qkv.at[0], s.cau_qkv.at[1], s.cau_qkv.at[2],
+        lambda scores, head: jnp.where(causal_live, scores, -jnp.inf), s.cau_p, s.cau_att,
+    )
+    loads["w_cau_out"].wait()
+    s.a_q[...] = mm(s.cau_att[...], s.w_cau_out[...])
+    pl.semaphore_wait(barrier, nb + 1)
+    a_q = send(s.a_q, s.a_q_in, core)
+
+    norm(R, RV, lambda ds: vis_ref[ds, :].astype(F32), 0, s.win_low, None, s.win_inv)
+    loads["w_win"].wait()
+    for i in range(3):
+        s.win_qkv[i] = mm(s.win_low[...], s.w_win[i]).astype(BF)
+    win_att = s.dyw.at[:, pl.ds(3 * H, H)]
+    attend(
+        s.win_qkv.at[0], s.win_qkv.at[1], s.win_qkv.at[2],
+        lambda scores, head: scores + s.bias[head], s.win_p, win_att,
+    )
+    loads["w_win_out"].wait()
+    s.a_v[...] = mm(win_att[...], s.w_win_out[...])
+    a_v = send(s.a_v, s.a_v_in, core)
+
+    a_q.wait_recv()
+    norm(
+        Q, RQ, lambda ds: query_ref[ds, :].astype(F32) + (s.a_q[ds, :] + s.a_q_in[ds, :]),
+        2, s.cq_low, s.cq_hat, s.cq_inv, s.que1,
+    )
+    loads["w_read"].wait()
+    loads["w_write"].wait()
+    s.read_q[...] = mm(s.cq_low[...], s.w_read[0]).astype(BF)
+    s.write_kv[0] = mm(s.cq_low[...], s.w_write[1]).astype(BF)
+    s.write_kv[1] = mm(s.cq_low[...], s.w_write[2]).astype(BF)
+    a_v.wait_recv()
+    norm(
+        R, RV, lambda ds: vis_ref[ds, :].astype(F32) + (s.a_v[ds, :] + s.a_v_in[ds, :]),
+        3, s.cv_low, s.cv_hat, s.cv_inv, s.vis1,
+    )
+    s.read_kv[0] = mm(s.cv_low[...], s.w_read[1]).astype(BF)
+    s.read_kv[1] = mm(s.cv_low[...], s.w_read[2]).astype(BF)
+    s.write_q[...] = mm(s.cv_low[...], s.w_write[0]).astype(BF)
+
+    stats = jnp.broadcast_to(jnp.where(lane < HEAD_DIM, 0.0, 1.0), (Q, 128))
+    for j in range(pairs):
+        at = columns(j)
+        qp, kp, vp = s.read_q[:, at], s.read_kv[0, :, at], s.read_kv[1, :, at]
+        halves = []
+        for t in range(2):
+            head = 2 * j + t
+            scores = mm_nt(qp * scaled[t], kp)
+            peak = jnp.max(scores, axis=-1, keepdims=True)
+            raised = jnp.exp(scores - peak)
+            s.read_p[head] = raised
+            stats = jnp.where(lane == head, peak, stats)
+            stats = jnp.where(lane == HEAD_DIM + head, jnp.sum(raised, axis=-1, keepdims=True), stats)
+            halves.append(mm(raised.astype(BF), vp))
+        s.part[:, at] = jnp.where(first, halves[0], halves[1])
+    s.part[:, H:] = stats
+
+    def own_rows(device):
+        return pl.ds(pl.multiple_of(device * own, own), own)
+
+    mine = own_rows(b)
+    part_copies = [send(s.part.at[own_rows(peer[1])], s.part_in.at[step], peer) for step, peer in enumerate(peers)]
+
+    att_w = s.dyc.at[:, pl.ds(3 * H, H)]
+    attend(
+        s.write_q, s.write_kv.at[0], s.write_kv.at[1],
+        lambda scores, head: jnp.where(alive, scores, -jnp.inf), s.write_p, att_w,
+    )
+    loads["w_write_out"].wait()
+    s.b_v[...] = mm(att_w[...], s.w_write_out[...])
+    b_v = send(s.b_v, s.b_v_in, core)
+
+    for copy in part_copies:
+        copy.wait_recv()
+    sources = [s.part.at[mine]] + [s.part_in.at[step] for step in range(nb - 1)]
+    peak = None
+    for source in sources:
+        peak = source[:, H:] if peak is None else jnp.maximum(peak, source[:, H:])
+    mass = jnp.zeros((own, 128), F32)
+    grown = []
+    for source in sources:
+        share = jnp.exp(source[:, H:] - peak)
+        grown.append(share)
+        mass = mass + share * pltpu.roll(source[:, H:], HEAD_DIM, 1)
+    known = lane < heads
+    mass = jnp.where(known, mass, 1.0)
+    over = 1.0 / mass
+    for j in range(pairs):
+        at = columns(j)
+        total = jnp.zeros((own, 128), F32)
+        for source, share in zip(sources, grown):
+            weight = share * over
+            total = total + source[:, at] * jnp.where(first, weight[:, 2 * j : 2 * j + 1], weight[:, 2 * j + 1 : 2 * j + 2])
+        s.mix[mine, at] = total
+    s.mix[mine, H:] = jnp.where(known, peak + jnp.log(mass), 0.0)
+    mix_copies = [send(s.mix.at[mine], s.mix.at[mine], peer) for peer in peers]
+
+    b_v.wait_recv()
+    norm(
+        R, RV, lambda ds: s.vis1[ds, :] + (s.b_v[ds, :] + s.b_v_in[ds, :]), 4, s.fv_low, s.fv_hat, s.fv_inv, s.vis2
+    )
+    loads["w_vdown"].wait()
+    loads["w_vup"].wait()
+    feed(s.fv_low, cotv_ref, s.w_up, s.w_down, s.dyf)
+    sent(a_v)
+    s.a_v[...] = mm_nt(s.dyf[:, :F], s.w_up[...])
+    d_v = send(s.a_v, s.a_v_in, core)
+    load("w_qup")
+    sent(b_v)
+    s.b_v[...] = mm(s.dyf[:, F:], s.w_down[...])
+    load("w_qdown")
+
+    for copy in mix_copies:
+        copy.wait_recv()
+    s.read_att[...] = s.mix[:, :H].astype(BF)
+    loads["w_read_out"].wait()
+    s.b_q[...] = mm(s.read_att[...], s.w_read_out[...])
+    b_q = send(s.b_q, s.b_q_in, core)
+
+    left((s.fv_low, cotv_ref), s.xf)
+    xf = send(s.x_out, s.xf_in, page)
+    dyf = send(s.dyf, s.dyf_in, page)
+
+    b_q.wait_recv()
+    norm(
+        Q, RQ, lambda ds: s.que1[ds, :] + (s.b_q[ds, :] + s.b_q_in[ds, :]), 5, s.fq_low, s.fq_hat, s.fq_inv, s.que2
+    )
+    loads["w_qdown"].wait()
+    loads["w_qup"].wait()
+    feed(s.fq_low, cotq_ref, s.w_up, s.w_down, s.dyq)
+    sent(a_q)
+    s.a_q[...] = mm_nt(s.dyq[:, :F], s.w_up[...])
+    d_q = send(s.a_q, s.a_q_in, core)
+
+    d_v.wait_recv()
+    norm_grad(
+        R, RV, lambda ds: cotv_ref[ds, :].astype(F32), (s.a_v, s.a_v_in), 4, s.fv_hat, s.fv_inv, s.vis1, s.gvis2_low
+    )
+    c_v = send(s.b_v, s.b_v_in, core)
+    s.da_v[...] = mm_nt(s.gvis2_low[...], s.w_write_out[...]).astype(BF)
+
+    def put_write(at, dq, dk, dv):
+        s.dyc[:, at] = dq.astype(BF)
+        s.qg[:, pl.ds(at.start + H, 128)] = dk
+        s.qg[:, pl.ds(at.start + 2 * H, 128)] = dv
+
+    attend_back(s.write_q, s.write_kv.at[0], s.write_kv.at[1], s.da_v, lambda head: s.write_p[head], put_write)
+
+    sent(b_q)
+    s.b_q[...] = mm(s.dyq[:, F:], s.w_down[...])
+    d_q.wait_recv()
+    norm_grad(
+        Q, RQ, lambda ds: cotq_ref[ds, :].astype(F32), (s.a_q, s.a_q_in), 5, s.fq_hat, s.fq_inv, s.que1, s.gque2_low
+    )
+    c_q = send(s.b_q, s.b_q_in, core)
+    s.da_q[...] = mm_nt(s.gque2_low[...], s.w_read_out[...]).astype(BF)
+
+    def read_prob(head):
+        moved = jnp.exp(s.part[:, H + head : H + head + 1] - s.mix[:, H + head : H + head + 1])
+        return s.read_p[head] * moved
+
+    def read_rowdot(dap, j, t):
+        return jnp.sum((dap * keep[t]).astype(F32) * s.mix[:, columns(j)], axis=-1, keepdims=True)
+
+    def put_read(at, dq, dk, dv):
+        s.qg[:, at] = dq
+        s.dyc[:, pl.ds(at.start + H, 128)] = dk.astype(BF)
+        s.dyc[:, pl.ds(at.start + 2 * H, 128)] = dv.astype(BF)
+
+    attend_back(s.read_q, s.read_kv.at[0], s.read_kv.at[1], s.da_q, read_prob, put_read, read_rowdot)
+    qg_copies = [send(s.qg.at[own_rows(peer[1])], s.qg_in.at[step], peer) for step, peer in enumerate(peers)]
+
+    c_v.wait_recv()
+    row_loop(R, RV, lambda ds: store(s.fv_low, ds, s.vis2[ds, :] + (s.b_v[ds, :] + s.b_v_in[ds, :])))
+    write(s.fv_low, vis_out)
+    sent(d_v)
+    s.a_v[...] = (
+        mm_nt(s.dyc[:, :H], s.w_write[0]) + mm_nt(s.dyc[:, H : 2 * H], s.w_read[1]) + mm_nt(s.dyc[:, 2 * H : 3 * H], s.w_read[2])
+    )
+    e_v = send(s.a_v, s.a_v_in, core)
+
+    f_panels = [s.w_down.at[pl.ds(n * half, half)] for n in range(4)]
+    c_panels = [s.w_up.at[pl.ds(0, half), pl.ds(n * D, D)] for n in range(2)]
+    w_panels = [s.w_up.at[pl.ds(half, half), pl.ds(n * D, D)] for n in range(2)]
+    xf.wait_recv()
+    dyf.wait_recv()
+    weight_grads(s.xf, s.xf_in, s.dyf, s.dyf_in, F, f_panels)
+    gf = side_push(f_panels, s.gf_in)
+    sent(xf)
+    left((s.cv_low, s.gvis2_low), s.xc)
+    xc = send(s.x_out, s.xc_in, page)
+    dyc = send(s.dyc, s.dyc_in, page)
+    query_grads(s.fq_low, s.dyq, 0, F, 0, s.tf, 0)
+    query_grads(cotq_ref, s.dyq, F, F, F, s.tf, F)
+    tf = send(s.tf, s.tf_in, page)
+
+    e_v.wait_recv()
+    norm_grad(R, RV, lambda ds: s.vis1[ds, :], (s.a_v, s.a_v_in), 3, s.cv_hat, s.cv_inv, s.vis1, s.gvis1_low)
+    s.da_v[...] = mm_nt(s.gvis1_low[...], s.w_win_out[...]).astype(BF)
+
+    def put_window(at, dq, dk, dv):
+        s.dyw[:, at] = dq.astype(BF)
+        s.dyw[:, pl.ds(at.start + H, 128)] = dk.astype(BF)
+        s.dyw[:, pl.ds(at.start + 2 * H, 128)] = dv.astype(BF)
+
+    def table_hook(head, ds):
+        s.bias[head] = ds
+
+    attend_back(
+        s.win_qkv.at[0], s.win_qkv.at[1], s.win_qkv.at[2], s.da_v, lambda head: s.win_p[head], put_window, hook=table_hook
+    )
+    sent(c_v)
+    s.b_v[...] = mm_nt(s.dyw[:, :H], s.w_win[0]) + mm_nt(s.dyw[:, H : 2 * H], s.w_win[1]) + mm_nt(s.dyw[:, 2 * H : 3 * H], s.w_win[2])
+    f_v = send(s.b_v, s.b_v_in, core)
+    sent(xc)
+    left((s.win_low, s.gvis1_low), s.xw)
+    xw = send(s.x_out, s.xw_in, page)
+    dyw = send(s.dyw, s.dyw_in, page)
+
+    for copy in qg_copies:
+        copy.wait_recv()
+    for c in range(3):
+        at = pl.ds(c * H, H)
+        total = s.qg[mine, at]
+        for step in range(nb - 1):
+            total = total + s.qg_in[step, :, at]
+        s.qg_low[mine, at] = total.astype(BF)
+    low_copies = [send(s.qg_low.at[mine], s.qg_low.at[mine], peer) for peer in peers]
+
+    s.strip[...] = jnp.zeros(s.strip.shape, F32)
+    for py in range(WIN):
+        at = (WIN - 1 - py) * WIN
+        s.strip[:, 0:WIN, at : at + AREA] += s.bias[:, py * WIN : (py + 1) * WIN, :]
+    for head in range(heads):
+        s.rolled[head] = split_dot(mm, s.strip[head], s.hot[...])
+    s.tab[...] = jnp.zeros(s.tab.shape, F32)
+    for head in range(heads):
+        total = s.rolled[head, 0:1, :]
+        for px in range(1, WIN):
+            total = total + pltpu.roll(s.rolled[head, px : px + 1, :], px, 1)
+        s.tab[head : head + 1, :] = total
+    tab = send(s.tab, s.tab_in, page)
+
+    for copy in gf:
+        copy.wait_recv()
+    zf = line_push(f_panels, s.gf_in, s.dyq, s.zf_in)
+
+    c_q.wait_recv()
+    row_loop(Q, RQ, lambda ds: store(s.fq_low, ds, s.que2[ds, :] + (s.b_q[ds, :] + s.b_q_in[ds, :])))
+    write(s.fq_low, query_out)
+    for copy in low_copies:
+        copy.wait_recv()
+    sent(d_q)
+    s.a_q[...] = (
+        mm_nt(s.qg_low[:, :H], s.w_read[0]) + mm_nt(s.qg_low[:, H : 2 * H], s.w_write[1]) + mm_nt(s.qg_low[:, 2 * H :], s.w_write[2])
+    )
+    e_q = send(s.a_q, s.a_q_in, core)
+    xc.wait_recv()
+    dyc.wait_recv()
+    weight_grads(s.xc, s.xc_in, s.dyc, s.dyc_in, 3 * H, c_panels)
+    gc = side_push(c_panels, s.gc_in)
+    e_q.wait_recv()
+    norm_grad(Q, RQ, lambda ds: s.que1[ds, :], (s.a_q, s.a_q_in), 2, s.cq_hat, s.cq_inv, s.que1, s.gque1_low)
+    s.da_q[...] = mm_nt(s.gque1_low[...], s.w_cau_out[...]).astype(BF)
+
+    def put_causal(at, dq, dk, dv):
+        s.cau_g[:, at] = dq.astype(BF)
+        s.cau_g[:, pl.ds(at.start + H, 128)] = dk.astype(BF)
+        s.cau_g[:, pl.ds(at.start + 2 * H, 128)] = dv.astype(BF)
+
+    attend_back(s.cau_qkv.at[0], s.cau_qkv.at[1], s.cau_qkv.at[2], s.da_q, lambda head: s.cau_p[head], put_causal)
+    sent(c_q)
+    s.b_q[...] = (
+        mm_nt(s.cau_g[:, :H], s.w_cau[0]) + mm_nt(s.cau_g[:, H : 2 * H], s.w_cau[1]) + mm_nt(s.cau_g[:, 2 * H :], s.w_cau[2])
+    )
+    f_q = send(s.b_q, s.b_q_in, core)
+
+    xw.wait_recv()
+    dyw.wait_recv()
+    weight_grads(s.xw, s.xw_in, s.dyw, s.dyw_in, 3 * H, w_panels)
+    gw = side_push(w_panels, s.gw_in)
+
+    base = 2 * F
+    query_grads(s.cq_low, s.qg_low, 0, 3 * H, base, s.tc, 0)
+    query_grads(s.gque2_low, s.read_att, 0, H, base + 3 * H, s.tc, 3 * H)
+    tc = send(s.tc, s.tc_in, page)
+    base = 2 * F + 4 * H
+    query_grads(s.cau_low, s.cau_g, 0, 3 * H, base, s.tw, 0)
+    query_grads(s.gque1_low, s.cau_att, 0, H, base + 3 * H, s.tw, 3 * H)
+    tw = send(s.tw, s.tw_in, page)
+
+    def hat_of(stream, inv):
+        return lambda ds: (stream[ds, :].astype(F32) - inv[ds, HEAD_DIM : HEAD_DIM + 1]) * inv[ds, 0:1]
+
+    f_v.wait_recv()
+    norm_grad(R, RV, lambda ds: s.vis1[ds, :], (s.b_v, s.b_v_in), 0, hat_of(vis_ref, s.win_inv), s.win_inv, s.vis1)
+    write(s.vis1, grad_vis)
+    f_q.wait_recv()
+    norm_grad(Q, RQ, lambda ds: s.que1[ds, :], (s.b_q, s.b_q_in), 1, hat_of(query_ref, s.cau_inv), s.cau_inv, s.que1)
+    write(s.que1, grad_query)
+    s.gain[6:8, :] = jnp.zeros((2, D), F32)
+    gain = send(s.gain, s.gain_in, page)
+
+    for copy in gc:
+        copy.wait_recv()
+    sent(dyf)
+    zc = line_push(c_panels, s.gc_in, s.dyf.at[:, pl.ds(0, 4 * H)], s.zc_in)
+
+    tab.wait_recv()
+    s.tab_page[...] = s.tab[...] + s.tab_in[...]
+    tab_copies = [send(s.tab_page, s.tab_blk.at[step], peer) for step, peer in enumerate(peers)]
+    gain.wait_recv()
+    s.gain_page[...] = s.gain[...] + s.gain_in[...]
+    gain_copies = [send(s.gain_page, s.gain_blk.at[step], peer) for step, peer in enumerate(peers)]
+
+    for copy in gw:
+        copy.wait_recv()
+    zw = line_push(w_panels, s.gw_in, s.dyf.at[:, pl.ds(4 * H, 4 * H)], s.zw_in)
+
+    for copy in zf:
+        copy.wait_recv()
+    line_sum(f_panels, s.gf_in, s.zf_in, 0)
+    tf.wait_recv()
+    add_query(s.tf_in, 0)
+    tc.wait_recv()
+    add_query(s.tc_in, 2 * F)
+    tw.wait_recv()
+    add_query(s.tw_in, 2 * F + 4 * H)
+    for copy in zc:
+        copy.wait_recv()
+    line_sum(c_panels, s.gc_in, s.zc_in, 2 * F)
+
+    for copy in tab_copies:
+        copy.wait_recv()
+    total = s.tab_page[...]
+    for step in range(nb - 1):
+        total = total + s.tab_blk[step]
+    table_out[...] = total
+    for copy in gain_copies:
+        copy.wait_recv()
+    total = s.gain_page[...]
+    for step in range(nb - 1):
+        total = total + s.gain_blk[step]
+    row = iota((8, 1), 0)
+    from_query = (row == 1) | (row == 2) | (row == 5)
+    total = jnp.where(from_query, s.gain_page[...], total)
+    pick = (iota((D, 128), 0) == iota((D, 128), 1) + (p * nb + b) * cut).astype(BF)
+    gain_out[...] = split_dot(mm, total, pick)
+
+    for copy in zw:
+        copy.wait_recv()
+    line_sum(w_panels, s.gw_in, s.zw_in, 2 * F + 4 * H)
+    for copy in list(started):
+        sent(copy)
+    for copy in written:
+        copy.wait()
+
+
+def finish_kernel(H, F, cut, *refs):
+    vis_in, query_in, gvis_in, gque_in, gain_in, slab_v, slab_q = refs[:7]
+    (
+        vis_out, query_out, gvis_out, gque_out, gain_out, win_qkv, win_out, cau_qkv, cau_out, read_qkv, read_out, write_qkv,
+        write_out, vis_up, vis_down, query_up, query_down,
+    ) = refs[7:]
+    vis_out[...] = vis_in[...]
+    query_out[...] = query_in[...]
+    gvis_out[...] = gvis_in[...]
+    gque_out[...] = gque_in[...]
+    gain_out[...] = gain_in[:6, :cut]
+
+    def turned(ref, at, size):
+        return jnp.transpose(ref[:, at : at + size], (1, 0))
+
+    vis_up[...] = slab_v[:, :F]
+    vis_down[...] = turned(slab_v, F, F)
+    query_up[...] = slab_q[:, :F]
+    query_down[...] = turned(slab_q, F, F)
+    cross, last = 2 * F, 2 * F + 4 * H
+    for i in range(3):
+        win_qkv[i] = slab_v[:, last + i * H : last + (i + 1) * H]
+        cau_qkv[i] = slab_q[:, last + i * H : last + (i + 1) * H]
+    win_out[...] = turned(slab_v, last + 3 * H, H)
+    cau_out[...] = turned(slab_q, last + 3 * H, H)
+    write_qkv[0] = slab_v[:, cross : cross + H]
+    read_qkv[1] = slab_v[:, cross + H : cross + 2 * H]
+    read_qkv[2] = slab_v[:, cross + 2 * H : cross + 3 * H]
+    write_out[...] = turned(slab_v, cross + 3 * H, H)
+    read_qkv[0] = slab_q[:, cross : cross + H]
+    write_qkv[1] = slab_q[:, cross + H : cross + 2 * H]
+    write_qkv[2] = slab_q[:, cross + 2 * H : cross + 3 * H]
+    read_out[...] = turned(slab_q, cross + 3 * H, H)
+
+
+ANY_SPEC = pl.BlockSpec(memory_space=pl.ANY)
+VMEM_SPEC = pl.BlockSpec(memory_space=pltpu.VMEM)
+
+
+def fused_shards(
+    vis_tokens, query_tokens, answer_lengths, norm_gains, bias_table, window_qkv, window_out, causal_qkv, causal_out,
+    read_qkv, read_out, write_qkv, write_out, vis_up, vis_down, query_up, query_down, cot_vis, cot_query,
+):
+    nb = lax.axis_size("blk")
+    R, D = vis_tokens.shape[1:]
+    Q = query_tokens.shape[1]
+    H, F = window_out.shape[0], vis_up.shape[1]
+    own, cut = Q // nb, D // (2 * nb)
+    heads = H // HEAD_DIM
+    table = jnp.pad(bias_table.reshape(heads, DIFFS * DIFFS), ((0, 8 - heads), (0, TABLE_LANES - DIFFS * DIFFS)))
+    scratch = scratch_shapes(R, Q, D, H, F, nb, own, cut)
+    names = tuple(scratch)
+    sems = 160
+    slab = jax.ShapeDtypeStruct((cut, 2 * F + 8 * H), F32)
+    shape = jax.ShapeDtypeStruct
+    pieces = pl.pallas_call(
+        partial(block_kernel, names, nb),
+        out_shape=(
+            shape((R, D), BF), shape((Q, D), BF), shape((R, D), F32), shape((Q, D), F32), shape((8, 128), F32),
+            shape((8, TABLE_LANES), F32), slab, slab,
+        ),
+        in_specs=[VMEM_SPEC, VMEM_SPEC, pl.BlockSpec(memory_space=pltpu.SMEM), VMEM_SPEC, VMEM_SPEC, VMEM_SPEC, VMEM_SPEC]
+        + [ANY_SPEC] * 12,
+        out_specs=[ANY_SPEC] * 4 + [VMEM_SPEC] * 2 + [ANY_SPEC] * 2,
+        scratch_shapes=[pltpu.VMEM(dims, dtype) for dims, dtype in scratch.values()]
+        + [pltpu.SemaphoreType.DMA((sems,)), pltpu.SemaphoreType.DMA((sems,)), pltpu.SemaphoreType.DMA((12,)), pltpu.SemaphoreType.DMA((16,))],
+        compiler_params=pltpu.CompilerParams(collective_id=0, has_side_effects=True, vmem_limit_bytes=VMEM_LIMIT),
+        name="block",
+    )(
+        vis_tokens[0], query_tokens[0], answer_lengths, norm_gains, table, cot_vis[0], cot_query[0], window_qkv, window_out,
+        causal_qkv, causal_out, read_qkv, read_out, write_qkv, write_out, vis_up, vis_down, query_up, query_down,
+    )
+    vis_part, query_part, gvis, gque, gain, tab, slab_v, slab_q = pieces
+    outs = pl.pallas_call(
+        partial(finish_kernel, H, F, cut),
+        out_shape=(
+            shape((R, D), BF), shape((Q, D), BF), shape((R, D), F32), shape((Q, D), F32), shape((6, cut), F32),
+            shape((3, cut, H), F32), shape((H, cut), F32), shape((3, cut, H), F32), shape((H, cut), F32),
+            shape((3, cut, H), F32), shape((H, cut), F32), shape((3, cut, H), F32), shape((H, cut), F32),
+            shape((cut, F), F32), shape((F, cut), F32), shape((cut, F), F32), shape((F, cut), F32),
+        ),
+        in_specs=[VMEM_SPEC] * 7,
+        out_specs=[VMEM_SPEC] * 17,
+        compiler_params=pltpu.CompilerParams(vmem_limit_bytes=VMEM_LIMIT),
+        name="finish",
+    )(vis_part, query_part, gvis, gque, gain, slab_v, slab_q)
+    table_grad = tab[:heads, : DIFFS * DIFFS].reshape(heads, DIFFS, DIFFS)
+    return (outs[0][None], outs[1][None], outs[2][None], outs[3][None], outs[4], table_grad) + tuple(outs[5:])
+
+
+VMEM_LIMIT = 60 * 2**20
 
 
 def combined_all(value, axis, join):
@@ -398,6 +1229,23 @@
     )
 
 
+def fits(mesh, args):
+    nb = mesh.shape["blk"]
+    rows, width = args[0].shape[1:]
+    queries = args[1].shape[1]
+    heads = args[4].shape[0]
+    return (
+        nb % 2 == 0
+        and mesh.shape["page"] == 2
+        and mesh.shape["head"] == 2
+        and rows == AREA * nb
+        and queries % (16 * nb) == 0
+        and width % (32 * nb) == 0
+        and heads % 4 == 0
+        and heads <= 16
+    )
+
+
 def solution(mesh):
     in_specs = (
         P("page", "blk", None),
@@ -440,4 +1288,9 @@
         P(("page", "blk"), "head"),
         P("head", ("page", "blk")),
     )
-    return jax.shard_map(shards, mesh=mesh, in_specs=in_specs, out_specs=out_specs, check_vma=False)
+
+    def step(*args):
+        body = fused_shards if fits(mesh, args) else shards
+        return jax.shard_map(body, mesh=mesh, in_specs=in_specs, out_specs=out_specs, check_vma=False)(*args)
+
+    return step

time: 2240 us -> 182 us (0.08)
  waiting for transfers between devices: 1720 us -> 0 us
  blocking collectives: 277 us -> 0 us
  Pallas kernels: 0 us -> 169 us
  matrix products: 116 us -> 0 us
  other arithmetic: 45.2 us -> 0 us
  local copies, waits for them, and re-layouts: 54.5 us -> 9.57 us
    reduce_scatter x12 -> x0, waiting for transfers between devices: 1620 us -> none  [the longest x1 143 us: shards(): lax.psum_scatter(query_down_grad, ('page', 'blk'), scatter_dimension=1, t...]
    psum x4 -> x0, blocking collectives: 215 us -> none  [the longest x1 78.6 us: shards(): table_part = lax.psum(table_grad, ('page', 'blk'))]
    pallas_call x0 -> x2, Pallas kernels: none -> 169 us  [the longest x1 164 us: fused_shards(): pl.pallas_call(partial(block_kernel, names, nb), out_shape=(shape((R, D),...]
    dot_general x88 -> x0, matrix products: 116 us -> none  [the longest x20 30.9 us: matmul(): return jnp.dot(matrix, other, preferred_element_type=jnp.float32)]
    psum x5 -> x0, waiting for transfers between devices: 97.1 us -> none  [head_total(): return lax.psum((first_part, second_part), 'head')]
    all_gather x2 -> x0, blocking collectives: 61.7 us -> none  [combined_all(): pieces = jax.tree.map(lambda part: lax.all_gather(part, axis), value)]
  transfers between devices with their start and end apart: 18 -> 0, of which waited for: 17 -> 0; matrix products, arithmetic and copies ran while one was open for 3% -> 0% of each run, Pallas kernels for 0% -> 0%
where the time goes in v1:
time: 182 us; the launch traced here: 180 us
  Pallas kernels  169 us (93%)
  local copies, waits for them, and re-layouts  9.57 us (5%)
    pallas_call x1, Pallas kernels, fused_shards(): pl.pallas_call(partial(block_kernel, names, nb), out_shape=(shape((R, D),...  164 us
    unnamed x16, local copies, waits for them, and re-layouts  7.26 us
    pallas_call x1, Pallas kernels, fused_shards(): pl.pallas_call(partial(finish_kernel, H, F, cut), out_shape=(shape((R, D)...  5.3 us

profile of v1, /device:TPU:0, one launch (start us, length us, event | category | flops | bytes accessed | tf_op | source)
XLA Modules:
  0.0 179.8 jit_solution(5835099458507015704)
XLA Ops:
  0.7 1.0 reshape.42
  1.6 0.6 pad.4.table_ref
  2.9 163.6 %block.1 = (bf16[144,768]{1,0:T(8,128)(2,1)}, bf16[256,768]{1,0:T(8,128)(2,1)}, f32[144,768]{1,0:T(8,128)}, f32[256,768]{1,0:T(8,128)}, f32[8,128]{1,0:T(8,128)}...) custom-call(bf16[144,768]{1,0:T(8,128)(2,1)} %bitcast.11, bf16[256,768]{1,0:T(8,128)(2,1)} %bitcast.9, ...), custom_call_target="tpu_custom_call" | custom-call | tf_op jit(solution)/shard_map/block/pallas_call | solution.py:810
  166.5 5.3 %finish.1 = (bf16[144,768]{1,0:T(8,128)(2,1)}, bf16[256,768]{1,0:T(8,128)(2,1)}, f32[144,768]{1,0:T(8,128)}, f32[256,768]{1,0:T(8,128)}, f32[6,48]{1,0:T(8,128)}...) custom-call(bf16[144,768]{1,0:T(8,128)(2,1)} %get-tuple-element.43.r, ...), custom_call_target="tpu_custom_call" | custom-call | tf_op jit(solution)/shard_map/finish/pallas_call | solution.py:828
  171.8 0.0 copy-start.3
  171.8 0.0 copy-start.2
  171.8 0.0 copy-start.1
  171.8 0.0 copy-start
  171.8 0.0 copy-start.4
  171.8 2.2 %copy.41 = f32[1536,48]{0,1:T(8,128)} copy(f32[1536,48]{1,0:T(8,128)} %get-tuple-element.83) | data formatting | bytes 589824
  174.0 2.1 %copy.42 = f32[1536,48]{0,1:T(8,128)} copy(f32[1536,48]{1,0:T(8,128)} %get-tuple-element.85) | data formatting | bytes 589824
  176.1 0.0 copy-done.3
  176.1 0.7 copy.37
  176.8 0.0 copy-done.2
  176.8 0.7 copy.38
  177.6 0.0 copy-done.1
  177.6 0.7 copy.39
  178.3 0.0 copy-done
  178.3 0.7 copy.40
  179.1 0.0 copy-done.4
  179.1 0.7 reshape.43
Async XLA Ops:
  171.8 4.3 %copy-start.3 = (f32[384,48]{1,0:T(8,128)S(1)}, f32[384,48]{1,0:T(8,128)}, u32[]{:S(2)}) copy-start(f32[384,48]{1,0:T(8,128)} %get-tuple-element.75) | copy-start | bytes 221188
  171.8 5.0 %copy-start.2 = (f32[384,48]{1,0:T(8,128)S(1)}, f32[384,48]{1,0:T(8,128)}, u32[]{:S(2)}) copy-start(f32[384,48]{1,0:T(8,128)} %get-tuple-element.77) | copy-start | bytes 221188
  171.8 5.8 %copy-start.1 = (f32[384,48]{1,0:T(8,128)S(1)}, f32[384,48]{1,0:T(8,128)}, u32[]{:S(2)}) copy-start(f32[384,48]{1,0:T(8,128)} %get-tuple-element.79) | copy-start | bytes 221188
  171.8 6.5 %copy-start = (f32[384,48]{1,0:T(8,128)S(1)}, f32[384,48]{1,0:T(8,128)}, u32[]{:S(2)}) copy-start(f32[384,48]{1,0:T(8,128)} %get-tuple-element.81) | copy-start | bytes 221188
  171.8 7.3 %copy-start.4 = (f32[8,640]{1,0:T(8,128)S(1)}, f32[8,640]{1,0:T(8,128)}, u32[]{:S(2)}) copy-start(f32[8,640]{1,0:T(8,128)} %get-tuple-element.55) | copy-start | bytes 61444
